TPU v7x, 128 devices: a whole 4x4x4 slice. The times are simulated.
128 devices in a mesh: fsdp: 16 (over y, z), tp: 8 (over x, core).
Axes of the slice: x: 4, y: 4, z: 4, core: 2. Of those that a mesh axis runs over, the one named last changes fastest.
Arguments:
- tokens: bfloat16 [4096, 4096], P('fsdp', 'tp'), may hold values from -6 to 6
- gate_tiles: bfloat16 [288, 1024, 128], P('fsdp', 'tp'), may hold values from -0.125 to 0.125
- up_tiles: bfloat16 [288, 1024, 128], P('fsdp', 'tp'), may hold values from -0.125 to 0.125
- gate_slots: int32 [288, 8], P(None, 'tp'), may hold values from -1 to 27, as said below
- up_slots: int32 [288, 8], P(None, 'tp'), may hold values from -1 to 27, as said below
- cotangent: bfloat16 [4096, 14336], P('fsdp', 'tp'), may hold values from -6 to 6
Outputs:
- hidden: bfloat16 [4096, 14336], P('fsdp', 'tp')
- input_grad: bfloat16 [4096, 4096], P('fsdp', 'tp')
- gate_tile_grad: bfloat16 [288, 1024, 128], P('fsdp', 'tp')
- up_tile_grad: bfloat16 [288, 1024, 128], P('fsdp', 'tp')
Inputs may be any that keep to these rules, and one draw needn't show every extreme that they name: `gate_slots`: for each owner (rows f * 18 to (f + 1) * 18 - 1, column t) the non-negative entries are distinct positions of that owner, stand before its -1 entries, and number 10 to 18; in every draw some owner fills all 18 slots. `up_slots`: as for gate_slots, drawn independently.
All inputs are finite; a program needn't handle non-finite values.
Results may differ from a plain program's by a relative error of at most 0.02.
Values may be sent and summed in bfloat16 or wider, within the bound.
No kernel may reach another device: no remote copies, remote signals or barrier semaphores. Data moves between devices by JAX's collectives and lax.ppermute only.
A program may use at most 192 MiB of HBM per device.

v0:
```python
import jax
import jax.numpy as jnp
from jax import lax
from jax.sharding import PartitionSpec as P


def per_device(tokens, gate_tiles, up_tiles, gate_slots, up_slots, cotangent):
    n_fsdp = lax.axis_size("fsdp")
    n_tp = lax.axis_size("tp")
    tile_size = gate_tiles.shape[-1]
    capacity = gate_tiles.shape[0]
    tok_rows = tokens.shape[0]
    gathered = lax.all_gather(tokens, "tp", axis=1, tiled=True)
    model_width = gathered.shape[1]
    ff_local = cotangent.shape[1]
    row_tiles = model_width // (tile_size * n_fsdp)
    col_tiles = ff_local // tile_size
    owner_tiles = row_tiles * col_tiles
    positions = jnp.arange(owner_tiles, dtype=jnp.int32)
    gate_table = gate_slots.reshape(n_fsdp, capacity)
    up_table = up_slots.reshape(n_fsdp, capacity)

    def selector(table, kind):
        picks = (table[:, :, None] == positions).astype(kind)
        return picks.reshape(table.shape[0], table.shape[1], row_tiles, col_tiles)

    gate_select = selector(gate_table, jnp.bfloat16)
    up_select = selector(up_table, jnp.bfloat16)
    gate_all, up_all = (
        lax.all_gather(gate_tiles, "fsdp", axis=0, tiled=True),
        lax.all_gather(up_tiles, "fsdp", axis=0, tiled=True),
    )

    def unpack(blocks, select):
        dense_tiles = jnp.einsum(
            "fcrj,fcab->frjab",
            select,
            blocks.reshape(n_fsdp, capacity, tile_size, tile_size),
            preferred_element_type=jnp.float32,
        )
        return dense_tiles.astype(jnp.bfloat16)

    w_gate = unpack(gate_all, gate_select)
    w_up = unpack(up_all, up_select)
    token_view = gathered.reshape(tok_rows, n_fsdp, row_tiles, tile_size)
    gate = jnp.einsum(
        "tfra,frjab->tjb", token_view, w_gate, preferred_element_type=jnp.float32
    ).reshape(tok_rows, ff_local)
    up = jnp.einsum(
        "tfra,frjab->tjb", token_view, w_up, preferred_element_type=jnp.float32
    ).reshape(tok_rows, ff_local)
    sigmoid_gate = jax.nn.sigmoid(gate)
    activated = gate * sigmoid_gate
    hidden = (activated * up).astype(jnp.bfloat16)
    upstream = cotangent.astype(jnp.float32)
    gate_grad = (upstream * up * sigmoid_gate * (1.0 + gate * (1.0 - sigmoid_gate))).astype(
        jnp.bfloat16
    )
    up_grad = (upstream * activated).astype(jnp.bfloat16)
    gate_view = gate_grad.reshape(tok_rows, col_tiles, tile_size)
    up_view = up_grad.reshape(tok_rows, col_tiles, tile_size)
    total = jnp.einsum(
        "frjab,tjb->frat", w_gate, gate_view, preferred_element_type=jnp.float32
    ) + jnp.einsum("frjab,tjb->frat", w_up, up_view, preferred_element_type=jnp.float32)
    input_part = lax.psum_scatter(
        total.reshape(model_width // n_tp * lax.axis_size("tp"), tok_rows).astype(jnp.bfloat16),
        "tp",
        scatter_dimension=0,
        tiled=True,
    ).astype(jnp.float32)
    input_grad = input_part.T.astype(jnp.bfloat16)
    gate_dense = jnp.einsum(
        "tfra,tjb->frajb", token_view, gate_view, preferred_element_type=jnp.float32
    ).astype(jnp.bfloat16)
    up_dense = jnp.einsum(
        "tfra,tjb->frajb", token_view, up_view, preferred_element_type=jnp.float32
    ).astype(jnp.bfloat16)
    gate_packed = jnp.einsum(
        "fcrj,frajb->fcab", gate_select, gate_dense, preferred_element_type=jnp.float32
    )
    up_packed = jnp.einsum(
        "fcrj,frajb->fcab", up_select, up_dense, preferred_element_type=jnp.float32
    )
    gate_packed = gate_packed.reshape(capacity * lax.axis_size("fsdp"), tile_size, tile_size)
    up_packed = up_packed.reshape(capacity * lax.axis_size("fsdp"), tile_size, tile_size)
    summed = lax.psum_scatter(
        jnp.concatenate([gate_packed, up_packed], axis=2).astype(jnp.bfloat16),
        "fsdp",
        scatter_dimension=0,
        tiled=True,
    ).astype(jnp.float32)
    gate_tile_grad = summed[:, :, :tile_size].astype(jnp.bfloat16)
    up_tile_grad = summed[:, :, tile_size:].astype(jnp.bfloat16)
    return (hidden, input_grad, gate_tile_grad, up_tile_grad)


def solution(mesh):
    placed = (
        P("fsdp", "tp"),
        P("fsdp", "tp", None),
        P("fsdp", "tp", None),
        P(None, "tp"),
        P(None, "tp"),
        P("fsdp", "tp"),
    )
    return jax.shard_map(
        per_device,
        mesh=mesh,
        in_specs=placed,
        out_specs=(P("fsdp", "tp"), P("fsdp", "tp"), P("fsdp", "tp", None), P("fsdp", "tp", None)),
        check_vma=False,
    )
```

profile of v0, /device:TPU:0, one launch (start us, length us, event | category | flops | bytes accessed | tf_op | source)
XLA Modules:
  0.0 513.8 jit_solution(2433849524178457601)
XLA Ops:
  7.2 0.0 all-gather.4.cloned.1.call-start
  7.2 0.7 all-gather.4.cloned.1.call-update
  7.9 0.0 all-gather.6.cloned.1.call-start
  7.9 1.8 copy.60
  9.7 0.0 all-gather.6.cloned.1.call-update
  9.8 0.0 all-gather.8.cloned.1.call-start
  9.8 0.7 all-gather.8.cloned.1.call-update
  10.5 0.0 reduce-scatter.5.cloned.1.call-start
  10.5 0.7 reduce
  11.2 0.7 reduce.1
  11.9 0.1 eq.49
  12.0 0.1 eq.42
  12.1 2.2 copy.67
  14.3 74.0 %all-gather.4.cloned.1.call-done = bf16[288,128,128]{2,1,0:T(8,128)(2,1)} async-done(((bf16[18,128,128]{2,1,0:T(8,128)(2,1)}), bf16[288,128,128]{2,1,0:T(8,128)(2,1)}) %all-gather.4.cloned.1.call-update) | async-done | bytes 9437200 | tf_op jit(solution)/shard_map/all_gather | solution.py:30
  88.4 16.0 %fusion.2 = bf16[16,2,14,128,128]{4,2,3,1,0:T(8,128)(2,1)} fusion(bf16[16,18,128,128,1]{3,2,1,0,4:T(8,128)(2,1)} %bitcast.119, s32[2,14]{1,0:T(2,128)S(1)} %multiply_add_fusion, s32[16,18]{1,0:T(8,128)S(1)} %eq.42), kind=kOutput, calls=%fused_computation.9 | convolution fusion | flops 264249216 | bytes 24118512 | tf_op jit(solution)/shard_map/fcrj,fcab->frjab/dot_general | solution.py:35
  104.4 11.0 %all-gather.6.cloned.1.call-done = bf16[256,4096]{0,1:T(8,128)(2,1)} async-done(((bf16[256,512]{0,1:T(8,128)(2,1)}), bf16[256,4096]{0,1:T(8,128)(2,1)}) %all-gather.6.cloned.1.call-update) | async-done | bytes 2097168 | tf_op jit(solution)/shard_map/all_gather | solution.py:13
  115.4 14.4 %fusion.6 = f32[14,128,256,1,1]{2,1,0,4,3:T(8,128)} fusion(bf16[256,16,2,128,1]{0,3,4,2,1:T(8,128)(2,1)} %bitcast.121, bf16[16,2,14,128,128]{4,2,3,1,0:T(8,128)(2,1)} %fusion.2), kind=kOutput, calls=%fused_computation.14 | convolution fusion | flops 3758096384 | bytes 18612224 | tf_op jit(solution)/shard_map/tfra,frjab->tjb/dot_general | solution.py:46
  129.8 63.8 %all-gather.8.cloned.1.call-done = bf16[288,128,128]{2,1,0:T(8,128)(2,1)} async-done(((bf16[18,128,128]{2,1,0:T(8,128)(2,1)}), bf16[288,128,128]{2,1,0:T(8,128)(2,1)}) %all-gather.8.cloned.1.call-update) | async-done | bytes 9437200 | tf_op jit(solution)/shard_map/all_gather | solution.py:31
  193.6 0.0 copy-start
  193.6 15.7 %fusion = bf16[16,2,14,128,128]{4,2,3,1,0:T(8,128)(2,1)} fusion(bf16[16,18,128,128,1]{3,2,1,0,4:T(8,128)(2,1)} %bitcast.120, s32[16,18]{1,0:T(8,128)S(1)} %eq.49, s32[2,14]{1,0:T(2,128)S(1)} %multiply_add_fusion), kind=kOutput, calls=%fused_computation.7 | convolution fusion | flops 264249216 | bytes 24118512 | tf_op jit(solution)/shard_map/fcrj,fcab->frjab/dot_general | solution.py:35
  209.4 0.0 copy-done
  209.4 0.0 copy-start.3
  209.4 13.6 %fusion.8 = f32[14,128,256,1,1]{2,1,0,4,3:T(8,128)S(1)} fusion(bf16[256,16,2,128,1]{0,3,4,2,1:T(8,128)(2,1)S(1)} %bitcast.122, bf16[16,2,14,128,128]{4,2,3,1,0:T(8,128)(2,1)} %fusion), kind=kOutput, calls=%fused_computation.16 | convolution fusion | flops 3758096384 | bytes 18612224 | tf_op jit(solution)/shard_map/tfra,frjab->tjb/dot_general | solution.py:49
  223.0 0.0 copy-done.3
  223.0 0.0 copy-done.4
  223.0 2.4 fusion.11
  225.3 7.2 %convert_bitcast_fusion = bf16[16,2,128,14,128]{2,4,1,0,3:T(8,128)(2,1)} fusion(bf16[256,14,128,1,1]{0,2,4,3,1:T(8,128)(2,1)S(1)} %bitcast.125, bf16[256,16,2,128,1]{0,3,2,1,4:T(8,128)(2,1)S(1)} %bitcast.123), kind=kOutput, calls=%fused_computation.5 | convolution fusion | flops 3765436416 | bytes 17694720 | tf_op jit(solution)/shard_map/tfra,tjb->frajb/dot_general | solution.py:75
  232.5 24.7 %copy.75 = bf16[16,2,128,14,128]{4,3,1,2,0:T(8,128)(2,1)} copy(bf16[16,2,128,14,128]{2,4,1,0,3:T(8,128)(2,1)} %convert_bitcast_fusion) | data formatting | bytes 29360128 | tf_op jit(solution)/shard_map/convert_element_type | solution.py:77
  257.2 10.2 %bitcast_convert_fusion = bf16[16,18,128,128]{3,1,2,0:T(8,128)(2,1)} fusion(bf16[16,2,128,14,128]{4,3,1,2,0:T(8,128)(2,1)} %copy.75, s32[16,18]{1,0:T(8,128)S(1)} %eq.49, s32[2,14]{1,0:T(2,128)S(1)} %multiply_add_fusion), kind=kOutput, calls=%fused_computation.2 | convolution fusion | flops 268967808 | bytes 24118512 | tf_op jit(solution)/shard_map/fcrj,frajb->fcab/dot_general | solution.py:81
  267.5 11.0 %copy.76 = bf16[16,18,128,128]{3,2,1,0:T(8,128)(2,1)} copy(bf16[16,18,128,128]{3,1,2,0:T(8,128)(2,1)} %bitcast_convert_fusion) | data formatting | bytes 18874368 | tf_op jit(solution)/shard_map/convert.4
  278.4 8.6 %convert_bitcast_fusion.1 = bf16[16,2,128,14,128]{2,4,1,0,3:T(8,128)(2,1)} fusion(bf16[256,14,128,1,1]{0,2,4,3,1:T(8,128)(2,1)} %bitcast.127, bf16[256,16,2,128,1]{0,3,2,1,4:T(8,128)(2,1)S(1)} %bitcast.124), kind=kOutput, calls=%fused_computation.6 | convolution fusion | flops 3765436416 | bytes 17694720 | tf_op jit(solution)/shard_map/tfra,tjb->frajb/dot_general | solution.py:72
  287.1 24.7 %copy.72 = bf16[16,2,128,14,128]{4,3,1,2,0:T(8,128)(2,1)} copy(bf16[16,2,128,14,128]{2,4,1,0,3:T(8,128)(2,1)} %convert_bitcast_fusion.1) | data formatting | bytes 29360128 | tf_op jit(solution)/shard_map/convert_element_type | solution.py:74
  311.8 10.4 %bitcast_convert_fusion.1 = bf16[16,18,128,128]{3,1,2,0:T(8,128)(2,1)} fusion(bf16[16,2,128,14,128]{4,3,1,2,0:T(8,128)(2,1)} %copy.72, s32[2,14]{1,0:T(2,128)S(1)} %multiply_add_fusion, s32[16,18]{1,0:T(8,128)S(1)} %eq.42), kind=kOutput, calls=%fused_computation.3 | convolution fusion | flops 268967808 | bytes 24118512 | tf_op jit(solution)/shard_map/fcrj,frajb->fcab/dot_general | solution.py:78
  322.2 11.0 %copy.73 = bf16[16,18,128,128]{3,2,1,0:T(8,128)(2,1)} copy(bf16[16,18,128,128]{3,1,2,0:T(8,128)(2,1)} %bitcast_convert_fusion.1) | data formatting | bytes 18874368 | tf_op jit(solution)/shard_map/convert.5
  333.2 16.8 %pad_maximum_fusion = bf16[288,128,256]{2,1,0:T(8,128)(2,1)} fusion(bf16[288,128,128]{2,1,0:T(8,128)(2,1)} %bitcast.117, bf16[288,128,128]{2,1,0:T(8,128)(2,1)} %bitcast.118), kind=kLoop, calls=%fused_computation.4 | loop fusion | flops 37748736 | bytes 37748736 | tf_op jit(solution)/shard_map/concatenate | solution.py:87
  350.0 0.0 reduce-scatter.5.cloned.1.call-update
  350.0 0.0 reduce-scatter.3.cloned.1.call-start
  350.1 1.1 copy-done.1
  351.2 9.3 %fusion.5 = f32[16,2,128,256,1]{3,2,4,1,0:T(8,128)S(1)} fusion(bf16[256,14,128,1,1]{0,2,1,4,3:T(8,128)(2,1)S(1)} %bitcast.128, bf16[16,2,14,128,128]{4,2,3,1,0:T(8,128)(2,1)} %fusion.2), kind=kOutput, calls=%fused_computation.13 | convolution fusion | flops 3758096384 | bytes 19791872 | tf_op jit(solution)/shard_map/frjab,tjb->frat/dot_general | solution.py:62
  360.5 0.0 copy-start.2
  360.5 10.7 %fusion.4 = bf16[16,2,128,256]{3,2,1,0:T(8,128)(2,1)} fusion(f32[16,2,128,256,1]{3,2,4,1,0:T(8,128)S(1)} %fusion.5, bf16[256,14,128,1,1]{0,2,1,4,3:T(8,128)(2,1)S(1)} %bitcast.126, bf16[16,2,14,128,128]{4,2,3,1,0:T(8,128)(2,1)} %fusion), kind=kOutput, calls=%fused_computation.12 | convolution fusion | flops 3760193536 | bytes 21889024 | tf_op jit(solution)/shard_map/frjab,tjb->frat/dot_general | solution.py:64
  371.2 4.1 copy.70
  375.3 0.0 reduce-scatter.3.cloned.1.call-update
  375.3 0.0 copy-done.2
  375.3 1.4 copy.77
  376.7 94.2 %reduce-scatter.5.cloned.1.call-done = bf16[18,128,256]{2,1,0:T(8,128)(2,1)} async-done(((bf16[288,128,256]{2,1,0:T(8,128)(2,1)}), bf16[18,128,256]{2,1,0:T(8,128)(2,1)}) %reduce-scatter.5.cloned.1.call-update) | async-done | bytes 1179664 | tf_op jit(solution)/shard_map/reduce_scatter | solution.py:86
  470.9 2.4 fusion.26
  473.3 33.8 %reduce-scatter.3.cloned.1.call-done = bf16[512,256]{0,1:T(8,128)(2,1)} async-done(((bf16[4096,256]{0,1:T(8,128)(2,1)}), bf16[512,256]{0,1:T(8,128)(2,1)}) %reduce-scatter.3.cloned.1.call-update) | async-done | bytes 262160 | tf_op jit(solution)/shard_map/reduce_scatter | solution.py:65
  (3 shorter events, 0.0 us)
Async XLA Ops:
  7.2 81.2 %all-gather.4.cloned.1.call-start = ((), (), s32[]{:S(2)}) async-start(), calls=%async_computation.2 | async-start | bytes 10027008 | tf_op jit(solution)/shard_map/all_gather | solution.py:30
  7.9 107.5 %all-gather.6.cloned.1.call-start = ((), (), s32[]{:S(2)}) async-start(), calls=%async_computation.3 | async-start | bytes 2359296 | tf_op jit(solution)/shard_map/all_gather | solution.py:13
  9.8 183.9 %all-gather.8.cloned.1.call-start = ((), (), s32[]{:S(2)}) async-start(), calls=%async_computation.4 | async-start | bytes 10027008 | tf_op jit(solution)/shard_map/all_gather | solution.py:31
  10.5 460.4 %reduce-scatter.5.cloned.1.call-start = ((), (), s32[]{:S(2)}) async-start(), calls=%async_computation.6 | async-start | bytes 20054016 | tf_op jit(solution)/shard_map/reduce_scatter | solution.py:86
  193.6 15.7 %copy-start = (bf16[256,4096]{0,1:T(8,128)(2,1)S(1)}, bf16[256,4096]{0,1:T(8,128)(2,1)}, u32[]{:S(2)}) copy-start(bf16[256,4096]{0,1:T(8,128)(2,1)} %all-gather.6.cloned.1.call-done) | copy-start | bytes 6291460
  209.4 13.6 %copy-start.3 = (bf16[256,1792]{0,1:T(8,128)(2,1)S(1)}, bf16[256,1792]{0,1:T(8,128)(2,1)}, u32[]{:S(2)}) copy-start(bf16[256,1792]{0,1:T(8,128)(2,1)} %copy.67) | copy-start | bytes 2752516
  209.4 13.6 %copy-start.4 = (f32[14,128,256,1,1]{2,1,0,4,3:T(8,128)S(1)}, f32[14,128,256,1,1]{2,1,0,4,3:T(8,128)}, u32[]{:S(2)}) copy-start(f32[14,128,256,1,1]{2,1,0,4,3:T(8,128)} %fusion.6) | copy-start | bytes 5505028
  350.0 1.2 copy-start.1
  350.0 157.1 %reduce-scatter.3.cloned.1.call-start = ((), (), s32[]{:S(2)}) async-start(), calls=%async_computation.5 | async-start | bytes 2359296 | tf_op jit(solution)/shard_map/reduce_scatter | solution.py:65
  360.5 14.9 %copy-start.2 = (bf16[256,1792]{0,1:T(8,128)(2,1)S(1)}, bf16[256,1792]{0,1:T(8,128)(2,1)}, u32[]{:S(2)}) copy-start(bf16[256,1792]{0,1:T(8,128)(2,1)} %get-tuple-element.17) | copy-start | bytes 2752516
Sparse Core Ops, SparseCore 0:
  10.2 78.1 all-gather.3
  90.7 24.6 all-gather.5
  117.6 75.9 all-gather.7
  350.1 120.7 reduce-scatter.4
  473.8 33.2 reduce-scatter.2
where the time goes:
time: 520 us; the launch traced here: 514 us
  waiting for transfers between devices  278 us (53%)
  matrix products  116 us (22%)
  local copies, waits for them, and re-layouts  84.6 us (16%)
  other arithmetic  20.6 us (4%)
  between operations  14.1 us (3%)
    reduce_scatter x1, waiting for transfers between devices, per_device(): lax.psum_scatter(jnp.concatenate([gate_packed, up_packed], axis=2).astype...  94.2 us
    all_gather x1, waiting for transfers between devices, per_device(): lax.all_gather(gate_tiles, 'fsdp', axis=0, tiled=True)  74 us
    all_gather x1, waiting for transfers between devices, per_device(): lax.all_gather(up_tiles, 'fsdp', axis=0, tiled=True)  63.8 us
    reduce_scatter x1, waiting for transfers between devices, per_device(): lax.psum_scatter(total.reshape(model_width // n_tp * lax.axis_size('tp'),...  33.8 us
    dot_general x2, matrix products, unpack(): jnp.einsum('fcrj,fcab->frjab', select, blocks.reshape(n_fsdp, capacity, t...  31.8 us
    convert_element_type x1, local copies, waits for them, and re-layouts, per_device(): up_dense = jnp.einsum('tfra,tjb->frajb', token_view, up_view, preferred_e...  24.7 us
    convert_element_type x1, local copies, waits for them, and re-layouts, per_device(): gate_dense = jnp.einsum('tfra,tjb->frajb', token_view, gate_view, preferr...  24.7 us
    another operation x2, local copies, waits for them, and re-layouts  21.9 us
  transfers between devices with their start and end apart: 5, of which 5 were waited for; matrix products, arithmetic and copies ran while one was open for 12% of the time, Pallas kernels for 0%

commit v1 on v0

--- a/solution.py
+++ b/solution.py
@@ -27,7 +27,12 @@
     gate_select = selector(gate_table, jnp.bfloat16)
     up_select = selector(up_table, jnp.bfloat16)
     gate_all, up_all = (
-        lax.all_gather(gate_tiles, "fsdp", axis=0, tiled=True),
+        jnp.concatenate(
+            lax.all_to_all(
+                jnp.stack([gate_tiles for _ in range(lax.axis_size("fsdp"))]), "fsdp", 0, 0
+            ),
+            0,
+        ),
         lax.all_gather(up_tiles, "fsdp", axis=0, tiled=True),
     )
 

time: 520 us -> 557 us (1.071)
  waiting for transfers between devices: 278 us -> 300 us
  starting transfers between devices: 0.2 us -> 8.47 us
  local copies, waits for them, and re-layouts: 84.6 us -> 90.7 us
    all_to_all x0 -> x1, waiting for transfers between devices: none -> 151 us  [per_device(): lax.all_to_all(jnp.stack([gate_tiles for _ in range(lax.axis_size('fsdp')...]
    all_gather x1 -> x0, waiting for transfers between devices: 74 us -> none  [per_device(): lax.all_gather(gate_tiles, 'fsdp', axis=0, tiled=True)]
    all_gather x1, waiting for transfers between devices: 63.8 us -> 15.8 us  [per_device(): lax.all_gather(up_tiles, 'fsdp', axis=0, tiled=True)]
    all_gather x1, waiting for transfers between devices: 11 us -> 0.02 us  [per_device(): gathered = lax.all_gather(tokens, 'tp', axis=1, tiled=True)]
    all_to_all x0 -> x1, starting transfers between devices: none -> 8.31 us  [per_device(): lax.all_to_all(jnp.stack([gate_tiles for _ in range(lax.axis_size('fsdp')...]
    another operation x2 -> x3, local copies, waits for them, and re-layouts: 21.9 us -> 29 us
  transfers between devices with their start and end apart: 5 -> 5, of which waited for: 5 -> 4; matrix products, arithmetic and copies ran while one was open for 12% -> 12% of each run, Pallas kernels for 0% -> 0%
where the time goes in v1:
time: 557 us; the launch traced here: 549 us
  waiting for transfers between devices  300 us (54%)
  matrix products  117 us (21%)
  local copies, waits for them, and re-layouts  90.7 us (16%)
  other arithmetic  19.2 us (3%)
  between operations  14.1 us (3%)
  starting transfers between devices  8.47 us (2%)
    all_to_all x1, waiting for transfers between devices, per_device(): lax.all_to_all(jnp.stack([gate_tiles for _ in range(lax.axis_size('fsdp')...  151 us
    reduce_scatter x1, waiting for transfers between devices, per_device(): lax.psum_scatter(jnp.concatenate([gate_packed, up_packed], axis=2).astype...  99 us
    reduce_scatter x1, waiting for transfers between devices, per_device(): lax.psum_scatter(total.reshape(model_width // n_tp * lax.axis_size('tp'),...  33.7 us
    dot_general x2, matrix products, unpack(): jnp.einsum('fcrj,fcab->frjab', select, blocks.reshape(n_fsdp, capacity, t...  31.8 us
    convert_element_type x1, local copies, waits for them, and re-layouts, per_device(): gate_dense = jnp.einsum('tfra,tjb->frajb', token_view, gate_view, preferr...  24.7 us
    convert_element_type x1, local copies, waits for them, and re-layouts, per_device(): up_dense = jnp.einsum('tfra,tjb->frajb', token_view, up_view, preferred_e...  24.7 us
    another operation x2, local copies, waits for them, and re-layouts  21.9 us
    concatenate x1, other arithmetic, per_device(): jnp.concatenate([gate_packed, up_packed], axis=2).astype(jnp.bfloat16)  16.8 us
  transfers between devices with their start and end apart: 5, of which 4 were waited for; matrix products, arithmetic and copies ran while one was open for 12% of the time, Pallas kernels for 0%

profile of v1, /device:TPU:0, one launch (start us, length us, event | category | flops | bytes accessed | tf_op | source)
XLA Modules:
  0.0 549.4 jit_solution(1958983056945469043)
XLA Ops:
  7.2 0.0 all-gather.3.cloned.1.call-start
  7.2 1.8 copy.61
  9.0 0.0 all-gather.3.cloned.1.call-update
  9.0 0.0 all-gather.5.cloned.1.call-start
  9.1 0.7 all-gather.5.cloned.1.call-update
  9.8 7.1 %stack.2 = bf16[16,18,128,128]{3,2,1,0:T(8,128)(2,1)} broadcast(bf16[18,128,128]{2,1,0:T(8,128)(2,1)} %param.7), dimensions={1,2,3} | broadcast | bytes 10027008 | tf_op jit(solution)/shard_map/stack | solution.py:32
  16.9 0.0 copy-start.6
  16.9 8.3 %all-to-all-start = ((bf16[16,18,128,128]{3,2,1,0:T(8,128)(2,1)}), bf16[16,18,128,128]{3,2,1,0:T(8,128)(2,1)}, u32[]{:S(2)}, u32[]{:S(2)}) async-start(bf16[16,18,128,128]{3,2,1,0:T(8,128)(2,1)} %stack.2), calls=%async_computation | async-start | bytes 18874368 | tf_op jit(solution)/shard_map/all_to_all | solution.py:31
  25.2 0.0 reduce-scatter.5.cloned.1.call-start
  25.3 0.0 copy-done.6
  25.3 0.0 copy-done.7
  25.3 0.1 eq.49
  25.4 0.1 eq.42
  25.5 0.0 copy-done.5
  25.5 1.3 copy.68
  26.8 150.8 %all-to-all-done = bf16[16,18,128,128]{3,2,1,0:T(8,128)(2,1)} async-done(((bf16[16,18,128,128]{3,2,1,0:T(8,128)(2,1)}), bf16[16,18,128,128]{3,2,1,0:T(8,128)(2,1)}, u32[]{:S(2)}, u32[]{:S(2)}) %all-to-all-start) | async-done | bytes 9437216 | tf_op jit(solution)/shard_map/all_to_all | solution.py:31
  177.7 16.0 %fusion.2 = bf16[16,2,14,128,128]{4,2,3,1,0:T(8,128)(2,1)} fusion(bf16[16,18,128,128,1]{3,2,1,0,4:T(8,128)(2,1)} %bitcast.2, s32[2,14]{1,0:T(2,128)S(1)} %multiply_add_fusion, s32[16,18]{1,0:T(8,128)S(1)} %eq.42), kind=kOutput, calls=%fused_computation.9 | convolution fusion | flops 264249216 | bytes 24118512 | tf_op jit(solution)/shard_map/fcrj,fcab->frjab/dot_general | solution.py:40
  193.7 0.0 all-gather.3.cloned.1.call-done
  193.7 14.7 %fusion.6 = f32[14,128,256,1,1]{2,1,0,4,3:T(8,128)} fusion(bf16[256,16,2,128,1]{0,3,4,2,1:T(8,128)(2,1)} %bitcast.118, bf16[16,2,14,128,128]{4,2,3,1,0:T(8,128)(2,1)} %fusion.2), kind=kOutput, calls=%fused_computation.14 | convolution fusion | flops 3758096384 | bytes 18612224 | tf_op jit(solution)/shard_map/tfra,frjab->tjb/dot_general | solution.py:51
  208.4 15.8 %all-gather.5.cloned.1.call-done = bf16[288,128,128]{2,1,0:T(8,128)(2,1)} async-done(((bf16[18,128,128]{2,1,0:T(8,128)(2,1)}), bf16[288,128,128]{2,1,0:T(8,128)(2,1)}) %all-gather.5.cloned.1.call-update) | async-done | bytes 9437200 | tf_op jit(solution)/shard_map/all_gather | solution.py:36
  224.3 15.7 %fusion = bf16[16,2,14,128,128]{4,2,3,1,0:T(8,128)(2,1)} fusion(bf16[16,18,128,128,1]{3,2,1,0,4:T(8,128)(2,1)} %bitcast.117, s32[16,18]{1,0:T(8,128)S(1)} %eq.49, s32[2,14]{1,0:T(2,128)S(1)} %multiply_add_fusion), kind=kOutput, calls=%fused_computation.7 | convolution fusion | flops 264249216 | bytes 24118512 | tf_op jit(solution)/shard_map/fcrj,fcab->frjab/dot_general | solution.py:40
  240.0 0.0 copy-done
  240.0 13.6 %fusion.8 = f32[14,128,256,1,1]{2,1,0,4,3:T(8,128)S(1)} fusion(bf16[256,16,2,128,1]{0,3,4,2,1:T(8,128)(2,1)S(1)} %bitcast.119, bf16[16,2,14,128,128]{4,2,3,1,0:T(8,128)(2,1)} %fusion), kind=kOutput, calls=%fused_computation.16 | convolution fusion | flops 3758096384 | bytes 18612224 | tf_op jit(solution)/shard_map/tfra,frjab->tjb/dot_general | solution.py:54
  253.6 0.0 copy-done.3
  253.6 0.0 copy-done.4
  253.6 2.4 fusion.11
  256.0 7.2 %convert_bitcast_fusion = bf16[16,2,128,14,128]{2,4,1,0,3:T(8,128)(2,1)} fusion(bf16[256,14,128,1,1]{0,2,4,3,1:T(8,128)(2,1)S(1)} %bitcast.122, bf16[256,16,2,128,1]{0,3,2,1,4:T(8,128)(2,1)S(1)} %bitcast.120), kind=kOutput, calls=%fused_computation.5 | convolution fusion | flops 3765436416 | bytes 17694720 | tf_op jit(solution)/shard_map/tfra,tjb->frajb/dot_general | solution.py:80
  263.2 24.7 %copy.76 = bf16[16,2,128,14,128]{4,3,1,2,0:T(8,128)(2,1)} copy(bf16[16,2,128,14,128]{2,4,1,0,3:T(8,128)(2,1)} %convert_bitcast_fusion) | data formatting | bytes 29360128 | tf_op jit(solution)/shard_map/convert_element_type | solution.py:82
  287.9 10.3 %bitcast_convert_fusion = bf16[16,18,128,128]{3,1,2,0:T(8,128)(2,1)} fusion(bf16[16,2,128,14,128]{4,3,1,2,0:T(8,128)(2,1)} %copy.76, s32[16,18]{1,0:T(8,128)S(1)} %eq.49, s32[2,14]{1,0:T(2,128)S(1)} %multiply_add_fusion), kind=kOutput, calls=%fused_computation.2 | convolution fusion | flops 268967808 | bytes 24118512 | tf_op jit(solution)/shard_map/fcrj,frajb->fcab/dot_general | solution.py:86
  298.2 10.9 %copy.77 = bf16[16,18,128,128]{3,2,1,0:T(8,128)(2,1)} copy(bf16[16,18,128,128]{3,1,2,0:T(8,128)(2,1)} %bitcast_convert_fusion) | data formatting | bytes 18874368 | tf_op jit(solution)/shard_map/convert.4
  309.1 8.6 %convert_bitcast_fusion.1 = bf16[16,2,128,14,128]{2,4,1,0,3:T(8,128)(2,1)} fusion(bf16[256,14,128,1,1]{0,2,4,3,1:T(8,128)(2,1)} %bitcast.124, bf16[256,16,2,128,1]{0,3,2,1,4:T(8,128)(2,1)S(1)} %bitcast.121), kind=kOutput, calls=%fused_computation.6 | convolution fusion | flops 3765436416 | bytes 17694720 | tf_op jit(solution)/shard_map/tfra,tjb->frajb/dot_general | solution.py:77
  317.8 24.7 %copy.73 = bf16[16,2,128,14,128]{4,3,1,2,0:T(8,128)(2,1)} copy(bf16[16,2,128,14,128]{2,4,1,0,3:T(8,128)(2,1)} %convert_bitcast_fusion.1) | data formatting | bytes 29360128 | tf_op jit(solution)/shard_map/convert_element_type | solution.py:79
  342.5 10.4 %bitcast_convert_fusion.1 = bf16[16,18,128,128]{3,1,2,0:T(8,128)(2,1)} fusion(bf16[16,2,128,14,128]{4,3,1,2,0:T(8,128)(2,1)} %copy.73, s32[2,14]{1,0:T(2,128)S(1)} %multiply_add_fusion, s32[16,18]{1,0:T(8,128)S(1)} %eq.42), kind=kOutput, calls=%fused_computation.3 | convolution fusion | flops 268967808 | bytes 24118512 | tf_op jit(solution)/shard_map/fcrj,frajb->fcab/dot_general | solution.py:83
  352.9 11.0 %copy.74 = bf16[16,18,128,128]{3,2,1,0:T(8,128)(2,1)} copy(bf16[16,18,128,128]{3,1,2,0:T(8,128)(2,1)} %bitcast_convert_fusion.1) | data formatting | bytes 18874368 | tf_op jit(solution)/shard_map/convert.5
  363.9 16.8 %pad_maximum_fusion = bf16[288,128,256]{2,1,0:T(8,128)(2,1)} fusion(bf16[288,128,128]{2,1,0:T(8,128)(2,1)} %bitcast.115, bf16[288,128,128]{2,1,0:T(8,128)(2,1)} %bitcast.116), kind=kLoop, calls=%fused_computation.4 | loop fusion | flops 37748736 | bytes 37748736 | tf_op jit(solution)/shard_map/concatenate | solution.py:92
  380.6 0.0 reduce-scatter.5.cloned.1.call-update
  380.7 0.0 reduce-scatter.3.cloned.1.call-start
  380.7 1.1 copy-done.1
  381.8 9.3 %fusion.5 = f32[16,2,128,256,1]{3,2,4,1,0:T(8,128)S(1)} fusion(bf16[256,14,128,1,1]{0,2,1,4,3:T(8,128)(2,1)S(1)} %bitcast.125, bf16[16,2,14,128,128]{4,2,3,1,0:T(8,128)(2,1)} %fusion.2), kind=kOutput, calls=%fused_computation.13 | convolution fusion | flops 3758096384 | bytes 19791872 | tf_op jit(solution)/shard_map/frjab,tjb->frat/dot_general | solution.py:67
  391.1 0.0 copy-start.2
  391.1 10.9 %fusion.4 = bf16[16,2,128,256]{3,2,1,0:T(8,128)(2,1)} fusion(f32[16,2,128,256,1]{3,2,4,1,0:T(8,128)S(1)} %fusion.5, bf16[256,14,128,1,1]{0,2,1,4,3:T(8,128)(2,1)S(1)} %bitcast.123, bf16[16,2,14,128,128]{4,2,3,1,0:T(8,128)(2,1)} %fusion), kind=kOutput, calls=%fused_computation.12 | convolution fusion | flops 3760193536 | bytes 21889024 | tf_op jit(solution)/shard_map/frjab,tjb->frat/dot_general | solution.py:69
  402.0 4.1 copy.71
  406.2 0.0 reduce-scatter.3.cloned.1.call-update
  406.2 0.0 copy-done.2
  406.2 1.4 copy.78
  407.6 99.0 %reduce-scatter.5.cloned.1.call-done = bf16[18,128,256]{2,1,0:T(8,128)(2,1)} async-done(((bf16[288,128,256]{2,1,0:T(8,128)(2,1)}), bf16[18,128,256]{2,1,0:T(8,128)(2,1)}) %reduce-scatter.5.cloned.1.call-update) | async-done | bytes 1179664 | tf_op jit(solution)/shard_map/reduce_scatter | solution.py:91
  506.6 2.4 fusion.26
  509.0 33.7 %reduce-scatter.3.cloned.1.call-done = bf16[512,256]{0,1:T(8,128)(2,1)} async-done(((bf16[4096,256]{0,1:T(8,128)(2,1)}), bf16[512,256]{0,1:T(8,128)(2,1)}) %reduce-scatter.3.cloned.1.call-update) | async-done | bytes 262160 | tf_op jit(solution)/shard_map/reduce_scatter | solution.py:70
  (9 shorter events, 0.1 us)
Async XLA Ops:
  7.2 186.6 %all-gather.3.cloned.1.call-start = ((), (), s32[]{:S(2)}) async-start(), calls=%async_computation.3 | async-start | bytes 2359296 | tf_op jit(solution)/shard_map/all_gather | solution.py:13
  9.0 215.2 %all-gather.5.cloned.1.call-start = ((), (), s32[]{:S(2)}) async-start(), calls=%async_computation.4 | async-start | bytes 10027008 | tf_op jit(solution)/shard_map/all_gather | solution.py:36
  16.9 8.4 %copy-start.6 = (s32[288,1]{0,1:T(1,128)S(1)}, s32[288,1]{0,1:T(1,128)}, u32[]{:S(2)}) copy-start(s32[288,1]{0,1:T(1,128)} %param.9) | copy-start | bytes 3460
  16.9 8.4 %copy-start.7 = (s32[288,1]{0,1:T(1,128)S(1)}, s32[288,1]{0,1:T(1,128)}, u32[]{:S(2)}) copy-start(s32[288,1]{0,1:T(1,128)} %param.10) | copy-start | bytes 3460
  16.9 8.6 %copy-start.5 = (bf16[256,1792]{1,0:T(8,128)(2,1)S(1)}, bf16[256,1792]{1,0:T(8,128)(2,1)}, u32[]{:S(2)}) copy-start(bf16[256,1792]{1,0:T(8,128)(2,1)} %param.11) | copy-start | bytes 2752516
  16.9 160.7 %all-to-all-start = ((bf16[16,18,128,128]{3,2,1,0:T(8,128)(2,1)}), bf16[16,18,128,128]{3,2,1,0:T(8,128)(2,1)}, u32[]{:S(2)}, u32[]{:S(2)}) async-start(bf16[16,18,128,128]{3,2,1,0:T(8,128)(2,1)} %stack.2), calls=%async_computation | async-start | bytes 18874368 | tf_op jit(solution)/shard_map/all_to_all | solution.py:31
  25.2 481.4 %reduce-scatter.5.cloned.1.call-start = ((), (), s32[]{:S(2)}) async-start(), calls=%async_computation.6 | async-start | bytes 20054016 | tf_op jit(solution)/shard_map/reduce_scatter | solution.py:91
  224.3 15.7 %copy-start = (bf16[256,4096]{0,1:T(8,128)(2,1)S(1)}, bf16[256,4096]{0,1:T(8,128)(2,1)}, u32[]{:S(2)}) copy-start(bf16[256,4096]{0,1:T(8,128)(2,1)} %all-gather.3.cloned.1.call-done) | copy-start | bytes 6291460
  240.0 13.6 %copy-start.3 = (bf16[256,1792]{0,1:T(8,128)(2,1)S(1)}, bf16[256,1792]{0,1:T(8,128)(2,1)}, u32[]{:S(2)}) copy-start(bf16[256,1792]{0,1:T(8,128)(2,1)} %copy.68) | copy-start | bytes 2752516
  240.0 13.6 %copy-start.4 = (f32[14,128,256,1,1]{2,1,0,4,3:T(8,128)S(1)}, f32[14,128,256,1,1]{2,1,0,4,3:T(8,128)}, u32[]{:S(2)}) copy-start(f32[14,128,256,1,1]{2,1,0,4,3:T(8,128)} %fusion.6) | copy-start | bytes 5505028
  380.6 1.2 copy-start.1
  380.7 162.0 %reduce-scatter.3.cloned.1.call-start = ((), (), s32[]{:S(2)}) async-start(), calls=%async_computation.5 | async-start | bytes 2359296 | tf_op jit(solution)/shard_map/reduce_scatter | solution.py:70
  391.1 15.1 %copy-start.2 = (bf16[256,1792]{0,1:T(8,128)(2,1)S(1)}, bf16[256,1792]{0,1:T(8,128)(2,1)}, u32[]{:S(2)}) copy-start(bf16[256,1792]{0,1:T(8,128)(2,1)} %get-tuple-element.17) | copy-start | bytes 2752516
Sparse Core Ops, SparseCore 0:
  10.3 27.5 all-gather.2
  40.1 184.1 all-gather.4
  380.8 125.7 reduce-scatter.4
  509.4 33.2 reduce-scatter.2
